TPU v7x, 256 devices: a whole 4x4x8 slice. The times are simulated.
256 devices in a mesh: dp: 32 (over z, x), vocab: 8 (over y, core).
Axes of the slice: x: 4, y: 4, z: 8, core: 2. Of those that a mesh axis runs over, the one named last changes fastest.
Arguments:
- hidden: bfloat16 [24576, 4096], P('dp'), may hold values from -8 to 8
- out_embed: bfloat16 [4096, 16384], P('dp', 'vocab'), may hold values from -1 to 1
- key_proj: bfloat16 [4096, 128], replicated, may hold values from -0.09375 to 0.09375
- targets: int32 [24576], P('dp'), may hold values from 0 to 16383
- doc_ids: int32 [24576], P('dp'), may hold values from 0 to 1
- list_owner: int32 [32, 64], P('dp'), may hold values from 0 to 31, as said below
- list_block: int32 [32, 64], P('dp'), may hold values from 0 to 5, as said below
- list_count: int32 [32], P('dp'), may hold values from 8 to 64, as said below
Outputs:
- row_loss: float32 [24576], P('dp')
Inputs may be any that keep to these rules, and one draw needn't show every extreme that they name: `list_owner`: among the first list_count[d] slots of row d at most 2 name the same owner; a row whose count is 64 names every owner exactly 2 times. Slots from list_count[d] on are ignored. `list_block`: live slots of one row that name the same owner name different blocks. `list_count`: some device's count is 64 in every draw.
All inputs are finite; a program needn't handle non-finite values.
Results may differ from a plain program's by a relative error of at most 0.0015.
Values may be sent and summed in bfloat16 or wider, within the bound.
A program may use at most 128 MiB of HBM per device.

v0:
```python
import jax
import jax.numpy as jnp
from jax import lax
from jax.sharding import PartitionSpec as P

KB = 128


negative_fill = -1e30
score_base = 3.0


def masked_stats(values, keep_mask):
    peak_value = jnp.max(jnp.where(keep_mask, values, negative_fill), axis=1)
    mass_value = jnp.sum(
        jnp.exp(jnp.where(keep_mask, values - peak_value[:, None], negative_fill)), axis=1
    )
    return (peak_value, mass_value)


def joined(earlier, later):
    peak_value = jnp.maximum(earlier[0], later[0])
    mass_value = earlier[1] * jnp.exp(earlier[0] - peak_value) + later[1] * jnp.exp(
        later[0] - peak_value
    )
    return (peak_value, mass_value)


def per_device(hidden, out_embed, key_proj, targets, doc_ids, list_owner, list_block, list_count):
    tok_dev = hidden.shape[0]
    shard_cols = out_embed.shape[1]
    vocab_count = lax.axis_size("vocab")
    dp_index = lax.axis_index("dp")
    vocab_index = lax.axis_index("vocab")
    block_count = tok_dev // KB
    slot_total = list_owner.shape[1]
    key_rows = jnp.dot(hidden, key_proj, preferred_element_type=jnp.float32).astype(jnp.bfloat16)
    key_width = key_rows.shape[1]
    sim_scale = score_base / key_width**0.5
    logits = jnp.dot(
        hidden,
        lax.all_gather(out_embed, "dp", axis=0, tiled=True),
        preferred_element_type=jnp.float32,
    )
    voc_peak = jnp.max(logits, axis=1)
    voc_mass = jnp.sum(jnp.exp(logits - voc_peak[:, None]), axis=1)
    local_tgt = targets - vocab_index * shard_cols
    column_ids = lax.broadcasted_iota(jnp.int32, (1, shard_cols), 1)
    voc_hit_peak, voc_hit_mass = masked_stats(logits, column_ids == local_tgt[:, None])
    row_share = tok_dev // vocab_count
    first_row = vocab_index * row_share
    query_rows = lax.dynamic_slice_in_dim(key_rows, first_row, row_share, 0)
    query_tgt = lax.dynamic_slice_in_dim(targets, first_row, row_share, 0)
    query_doc = lax.dynamic_slice_in_dim(doc_ids, first_row, row_share, 0)
    query_pos = dp_index * tok_dev + first_row + jnp.arange(row_share, dtype=jnp.int32)
    offsets = jnp.arange(KB, dtype=jnp.int32)
    owners = list_owner[0]
    blocks = list_block[0]
    live_slot = jnp.arange(slot_total, dtype=jnp.int32) < list_count[0]
    every_key, every_tgt, every_doc = (
        lax.all_gather(key_rows, "dp", axis=0, tiled=True),
        lax.all_gather(targets, "dp", axis=0, tiled=True),
        lax.all_gather(doc_ids, "dp", axis=0, tiled=True),
    )
    slot_ids = owners * block_count + blocks
    mem_rows = every_key.reshape(-1, KB, key_width)[slot_ids].reshape(-1, key_width)
    mem_tgt = every_tgt.reshape(-1, KB)[slot_ids].reshape(-1)
    mem_doc = every_doc.reshape(-1, KB)[slot_ids].reshape(-1)
    mem_pos = (slot_ids[:, None] * KB + offsets[None, :]).reshape(-1)
    key_live = jnp.repeat(live_slot, KB)
    scores = sim_scale * lax.dot_general(
        query_rows, mem_rows, (((1,), (1,)), ((), ())), preferred_element_type=jnp.float32
    )
    keep_mask = (
        key_live[None, :]
        & (mem_doc[None, :] == query_doc[:, None])
        & (mem_pos[None, :] != query_pos[:, None])
    )
    mem_peak, mem_mass = masked_stats(scores, keep_mask)
    hit_mask = keep_mask & (mem_tgt[None, :] == query_tgt[:, None])
    mem_hit_peak, mem_hit_mass = masked_stats(scores, hit_mask)

    def spread(values, filler):
        return lax.dynamic_update_slice(
            jnp.full((tok_dev,), filler, jnp.float32), values, (first_row,)
        )

    peak_value, mass_value = joined(
        (voc_peak, voc_mass), (spread(mem_peak, negative_fill), spread(mem_mass, 0.0))
    )
    hit_peak, hit_mass = joined(
        (voc_hit_peak, voc_hit_mass),
        (spread(mem_hit_peak, negative_fill), spread(mem_hit_mass, 0.0)),
    )
    top_peak, top_hit = lax.pmax((peak_value, hit_peak), "vocab")
    sum_mass, sum_hit = lax.psum(
        (mass_value * jnp.exp(peak_value - top_peak), hit_mass * jnp.exp(hit_peak - top_hit)),
        "vocab",
    )
    return top_peak + jnp.log(sum_mass) - top_hit - jnp.log(sum_hit)


def solution(mesh):
    placed = (
        P("dp", None),
        P("dp", "vocab"),
        P(),
        P("dp"),
        P("dp"),
        P("dp", None),
        P("dp", None),
        P("dp"),
    )
    return jax.shard_map(per_device, mesh=mesh, in_specs=placed, out_specs=P("dp"), check_vma=False)
```

profile of v0, /device:TPU:1, one launch (start us, length us, event | category | flops | bytes accessed | tf_op | source)
XLA Modules:
  0.0 301.9 jit_solution(13907528438665449179)
XLA Ops:
  6.6 1.2 copy-done
  7.8 5.2 %convolution_convert_fusion = bf16[768,128]{1,0:T(8,128)(2,1)} fusion(bf16[768,4096]{1,0:T(8,128)(2,1)} %param.8, bf16[4096,128]{1,0:T(8,128)(2,1)S(1)} %copy-done), kind=kOutput, calls=%fused_computation.14 | convolution fusion | flops 805404672 | bytes 7536640 | tf_op jit(solution)/shard_map/dot_general | solution.py:37
  13.1 0.7 all-gather.5.cloned.1.call-update
  13.8 0.1 dynamic_slice.9
  13.9 0.1 dynamic_slice.11
  14.6 39.3 %all-gather = s32[32,1,768]{2,1,0:T(1,128)S(1)} all-gather(s32[1,1,768]{2,1,0:T(1,128)S(1)} %reshape.113), channel_id=1, replica_groups=mesh['dp'=32,'vocab'=8] {'dp'}, dimensions={0}, use_global_device_ids=true | all-gather | bytes 101376 | tf_op jit(solution)/shard_map/all_gather | solution.py:63
  54.0 0.6 gather_fusion
  54.6 35.6 %all-gather.1 = s32[32,1,768]{2,1,0:T(1,128)S(1)} all-gather(s32[1,1,768]{2,1,0:T(1,128)S(1)} %reshape.115), channel_id=1, replica_groups=mesh['dp'=32,'vocab'=8] {'dp'}, dimensions={0}, use_global_device_ids=true | all-gather | bytes 101376 | tf_op jit(solution)/shard_map/all_gather | solution.py:62
  90.2 0.6 gather_fusion.2
  90.9 0.1 broadcast_bitcast_fusion
  91.0 14.4 %all-gather.7.cloned.1.call-done = bf16[24576,128]{1,0:T(8,128)(2,1)} async-done(((bf16[768,128]{1,0:T(8,128)(2,1)}), bf16[24576,128]{1,0:T(8,128)(2,1)}) %all-gather.7.cloned.1.call-update) | async-done | bytes 6291472 | tf_op jit(solution)/shard_map/all_gather | solution.py:61
  105.4 3.7 %gather_fusion.1 = bf16[64,128,128]{2,1,0:T(8,128)(2,1)S(1)} fusion(bf16[192,128,128]{2,1,0:T(8,128)(2,1)} %bitcast.26, s32[1024]{0:T(1024)S(1)} %pad_clamp_fusion), kind=kCustom, calls=%fused_computation.1 | custom fusion | bytes 4194560 | tf_op jit(solution)/shard_map/gather | solution.py:66
  109.1 4.5 %select_reduce_fusion.2 = (f32[96]{0:T(128)S(1)}, f32[96]{0:T(128)S(1)}, f32[96,8192]{1,0:T(8,128)}) fusion(s32[96]{0:T(128)S(1)} %iota_add_fusion, s32[8192]{0:T(1024)S(1)} %add_bitcast_fusion, s32[96]{0:T(128)S(1)} %dynamic_slice.9, s32[8192]{0:T(1024)S(1)} %bitcast.27, pred[8192]{0:T(1024)(128)(4,1)S(1)} %broadcast_bitcast_fusion, ...), kind=kOutput, calls=%fused_computation.11 | convolution fusion | flops 209977152 | bytes 5375876 | tf_op jit(solution)/shard_map/dot_general | solution.py:71
  113.6 0.2 dynamic_update_slice.14
  113.9 0.2 dynamic_update_slice.12
  114.1 3.8 %exponential_reduce_fusion.3 = (f32[96]{0:T(128)S(1)}, f32[96]{0:T(128)S(1)}) fusion(f32[96,8192]{1,0:T(8,128)} %get-tuple-element.18, f32[96]{0:T(128)S(1)} %get-tuple-element.11, s32[96]{0:T(128)S(1)} %iota_add_fusion, s32[8192]{0:T(1024)S(1)} %add_bitcast_fusion, s32[96]{0:T(128)S(1)} %dynamic_slice.9, s32[8192]{0:T(1024)S(1)} %bitcast.28, ...), kind=kLoop, calls=%fused_computation.10 | loop fusion | flops 9436992 | bytes 3254912 | tf_op jit(solution)/shard_map/reduce_sum | solution.py:15
  118.0 0.2 dynamic_update_slice.15
  118.2 0.2 dynamic_update_slice.13
  118.4 127.4 %all-gather.5.cloned.1.call-done = bf16[4096,2048]{1,0:T(8,128)(2,1)} async-done(((bf16[128,2048]{1,0:T(8,128)(2,1)}), bf16[4096,2048]{1,0:T(8,128)(2,1)}) %all-gather.5.cloned.1.call-update) | async-done | bytes 16777232 | tf_op jit(solution)/shard_map/all_gather | solution.py:42
  245.8 18.3 %fusion.3 = (f32[768]{0:T(1024)S(1)}, f32[768]{0:T(1024)S(1)}, f32[768,2048]{1,0:T(8,128)S(1)}) fusion(s32[768]{0:T(1024)S(1)} %broadcast_subtract_fusion, bf16[768,4096]{1,0:T(8,128)(2,1)} %param.8, bf16[4096,2048]{1,0:T(8,128)(2,1)} %all-gather.5.cloned.1.call-done), kind=kOutput, calls=%fused_computation.30 | convolution fusion | flops 12891191296 | bytes 29369344 | tf_op jit(solution)/shard_map/dot_general | solution.py:40
  264.2 2.7 exponential_reduce_fusion.1
  266.9 13.0 %all-reduce.1 = (f32[768]{0:T(1024)S(1)}, f32[768]{0:T(1024)S(1)}) all-reduce(f32[768]{0:T(1024)S(1)} %max.11, f32[768]{0:T(1024)S(1)} %max.10), channel_id=1, replica_groups=mesh['dp'=32,'vocab'=8] {'vocab'}, use_global_device_ids=true, to_apply=%region_8.9 | all-reduce | flops 1536 | bytes 12288 | tf_op jit(solution)/shard_map/pmax | solution.py:95
  279.9 14.5 %all-reduce = (f32[768]{0:T(1024)S(1)}, f32[768]{0:T(1024)S(1)}) all-reduce(f32[768]{0:T(1024)S(1)} %get-tuple-element.19, f32[768]{0:T(1024)S(1)} %get-tuple-element.20), channel_id=1, replica_groups=mesh['dp'=32,'vocab'=8] {'vocab'}, use_global_device_ids=true, to_apply=%region_11.12 | all-reduce | flops 1536 | bytes 12288 | tf_op jit(solution)/shard_map/psum | solution.py:96
  294.4 0.6 log_subtract_fusion
  (28 shorter events, 0.3 us)
Async XLA Ops:
  6.5 1.2 copy-start
  6.5 7.2 %copy-start.2 = (s32[768]{0:T(1024)S(1)}, s32[768]{0:T(1024)}, u32[]{:S(2)}) copy-start(s32[768]{0:T(1024)} %param.12) | copy-start | bytes 9220
  6.5 7.3 %copy-start.1 = (s32[768]{0:T(1024)S(1)}, s32[768]{0:T(1024)}, u32[]{:S(2)}) copy-start(s32[768]{0:T(1024)} %param.11) | copy-start | bytes 9220
  6.5 47.4 %copy-start.3 = (s32[1,64]{1,0:T(1,128)S(1)}, s32[1,64]{1,0:T(1,128)}, u32[]{:S(2)}) copy-start(s32[1,64]{1,0:T(1,128)} %param.14) | copy-start | bytes 772
  6.5 47.4 %copy-start.4 = (s32[1,64]{1,0:T(1,128)S(1)}, s32[1,64]{1,0:T(1,128)}, u32[]{:S(2)}) copy-start(s32[1,64]{1,0:T(1,128)} %param.13) | copy-start | bytes 772
  6.5 98.8 %all-gather.7.cloned.1.call-start = ((), (), s32[]{:S(2)}) async-start(), calls=%async_computation.1 | async-start | bytes 6488064 | tf_op jit(solution)/shard_map/all_gather | solution.py:61
  13.0 232.8 %all-gather.5.cloned.1.call-start = ((), (), s32[]{:S(2)}) async-start(), calls=%async_computation | async-start | bytes 17301504 | tf_op jit(solution)/shard_map/all_gather | solution.py:42
Sparse Core Ops, SparseCore 0:
  13.1 92.1 all-gather.6
  108.0 137.7 all-gather.4
where the time goes:
time: 302 us
  waiting for transfers between devices  142 us (47%)
  blocking collectives  102 us (34%)
  matrix products  28.1 us (9%)
  between operations  14.2 us (5%)
  other arithmetic  7.3 us (2%)
  local copies, waits for them, and re-layouts  7.27 us (2%)
    all_gather x1, waiting for transfers between devices, per_device(): lax.all_gather(out_embed, 'dp', axis=0, tiled=True)  127 us
    all_gather x1, blocking collectives, per_device(): lax.all_gather(doc_ids, 'dp', axis=0, tiled=True)  39.3 us
    all_gather x1, blocking collectives, per_device(): lax.all_gather(targets, 'dp', axis=0, tiled=True)  35.6 us
    dot_general x1, matrix products, per_device(): jnp.dot(hidden, lax.all_gather(out_embed, 'dp', axis=0, tiled=True), pref...  18.3 us
    psum x1, blocking collectives, per_device(): lax.psum((mass_value * jnp.exp(peak_value - top_peak), hit_mass * jnp.exp...  14.5 us
    all_gather x1, waiting for transfers between devices, per_device(): lax.all_gather(key_rows, 'dp', axis=0, tiled=True)  14.4 us
    pmax x1, blocking collectives, per_device(): top_peak, top_hit = lax.pmax((peak_value, hit_peak), 'vocab')  13 us
  transfers between devices with their start and end apart: 2, of which 2 were waited for; matrix products, arithmetic and copies ran while one was open for 5% of the time, Pallas kernels for 0%

commit v1 on v0

v1 whole, which is shorter than its diff:
```python
import jax
import jax.numpy as jnp
from jax import lax
from jax.experimental import pallas as pl
from jax.experimental.pallas import tpu as pltpu
from jax.sharding import PartitionSpec as P

MESH = pl.DeviceIdType.MESH
NEG = -1e30
SCALE = 3.0 / 128**0.5
NX, NY, NZ = 4, 4, 8
CHUNK = 32
F32 = jnp.float32
BF16 = jnp.bfloat16


def kernel(
    hid, emb, kproj, tgt, doc, lown, lblk, lcnt, out,
    hb, eb, kp, lg, kv, mt, om, kg, kt, kd, ko, ms, st, r1, st2, r2,
    loc_sem, xe_s, xe_r, zp_s, zp_r, zm_s, zm_r, dc_s, dc_r,
    hx_s, hf_s, hx_r, yp_s, ym_s, yp_r, ym_r, yf_s, yf_r,
    kv_s, kv_r, om_s, om_r, kc_s, kc_r, mt_s, mt_r, r1_s, r1_r, r2_s, r2_r,
):
    d = lax.axis_index("dp")
    v = lax.axis_index("vocab")
    z, x = d // NX, d % NX
    y, c = v // 2, v % 2
    owner_here = z % NY == y
    first, second = c == 0, c == 1

    def tok_x(s):
        return (x + 3 * c + 2 * s) % NX

    def dev(dz, dx, dy, dc):
        return (((z + dz) % NZ) * NX + (x + dx) % NX, ((y + dy) % NY) * 2 + (c + dc) % 2)

    def rcopy(src, dst, ssem, rsem, to):
        return pltpu.make_async_remote_copy(
            src_ref=src, dst_ref=dst, send_sem=ssem, recv_sem=rsem, device_id=to, device_id_type=MESH
        )

    bar = pltpu.get_barrier_semaphore()
    for to in [dev(1, 0, 0, 0), dev(NZ - 1, 0, 0, 0)] + [
        dev(0, 1, 0, 0), dev(0, 2, 0, 0), dev(0, 3, 0, 0), dev(0, 1, 0, 1), dev(0, 3, 0, 1)
    ]:
        pl.semaphore_signal(bar, inc=1, device_id=to, device_id_type=MESH)
    for n in range(1, 8):
        pl.semaphore_signal(bar, inc=1, device_id=(d, (v + n) % 8), device_id_type=MESH)

    om_loads = []
    for n in range(6):
        om_loads.append(pltpu.make_async_copy(tgt.at[pl.ds(n * 128, 128)], om.at[2, n], loc_sem.at[4]))
        om_loads.append(pltpu.make_async_copy(doc.at[pl.ds(n * 128, 128)], om.at[2, 6 + n], loc_sem.at[4]))
    for cp in om_loads:
        cp.start()
    emb_loads = []
    for ph in range(2):
        col = pl.multiple_of(x * 512 + ph * 256, 256)
        cp = pltpu.make_async_copy(
            emb.at[:, pl.ds(col, 256)], eb.at[ph, c, pl.ds(pl.multiple_of(d * 128, 128), 128)], loc_sem.at[2 + ph]
        )
        cp.start()
        emb_loads.append(cp)
    own_slot = 2 * c
    kp_load = pltpu.make_async_copy(kproj, kp, loc_sem.at[1])
    kp_load.start()
    hid_load = pltpu.make_async_copy(hid, hb.at[own_slot], loc_sem.at[0])
    hid_load.start()
    om[2, 12:16] = jnp.zeros((4, 128), jnp.int32)
    om[2, 12:13, 0:64] = lown[...]
    om[2, 13:14, 0:64] = lblk[...]
    om[2, 14:15] = jnp.full((1, 128), lcnt[0], jnp.int32)
    pl.semaphore_wait(bar, 14)

    def eslot(ph, zz, i):
        row = ((zz % NZ) * NX + (x + i) % NX) * 128
        return eb.at[ph, c, pl.ds(pl.multiple_of(row, 128), 128)]

    def xe(ph, e):
        col = pl.multiple_of(((x + e) % NX) * 512 + ph * 256, 256)
        return rcopy(
            emb.at[:, pl.ds(col, 256)],
            eb.at[ph, c, pl.ds(pl.multiple_of(d * 128, 128), 128)],
            xe_s.at[ph, e], xe_r.at[ph, 4 - e], dev(0, e, 0, 0),
        )

    def xe_in(ph, i):
        return rcopy(
            emb.at[:, pl.ds(0, 256)], eslot(ph, z, i), xe_s.at[ph, i], xe_r.at[ph, i], dev(0, i, 0, 0)
        )

    def zplus(ph, s, i):
        ref = eslot(ph, z - (s - 1) + NZ, i)
        return rcopy(ref, ref, zp_s.at[ph, s - 1, i], zp_r.at[ph, s - 1, i], dev(1, 0, 0, 0))

    def zminus(ph, s, i):
        ref = eslot(ph, z + (s - 1), i)
        return rcopy(ref, ref, zm_s.at[ph, s - 1, i], zm_r.at[ph, s - 1, i], dev(NZ - 1, 0, 0, 0))

    def zplus_in(ph, s, i):
        ref = eslot(ph, z - s + NZ, i)
        return rcopy(ref, ref, zp_s.at[ph, s - 1, i], zp_r.at[ph, s - 1, i], dev(1, 0, 0, 0))

    def zminus_in(ph, s, i):
        ref = eslot(ph, z + s, i)
        return rcopy(ref, ref, zm_s.at[ph, s - 1, i], zm_r.at[ph, s - 1, i], dev(NZ - 1, 0, 0, 0))

    def d2d(ph, zz, n, shard):
        ref = eb.at[ph, shard, pl.ds(pl.multiple_of((zz % NZ) * 512, 512), 512)]
        return rcopy(ref, ref, dc_s.at[ph, n], dc_r.at[ph, n], dev(0, 0, 0, 1))

    d2d_z = [0, 7, 6, 5, 1, 2, 3, 4]

    def z_first(ph, pair):
        for i in ((0,), (1,), (2, 3))[pair]:
            if i == 0:
                emb_loads[ph].wait()
            else:
                xe_in(ph, i).wait_recv()
            zplus(ph, 1, i).start()
            zminus(ph, 1, i).start()
        if pair == 2:
            d2d(ph, z, 0, c).start()

    def z_event(ph, s, pair):
        if s < 4:
            for i in (0, 1) if pair == 0 else (2, 3):
                zplus_in(ph, s, i).wait_recv()
                if s < 3 or i < 2:
                    zplus(ph, s + 1, i).start()
                zminus_in(ph, s, i).wait_recv()
                if s < 3 or i >= 2:
                    zminus(ph, s + 1, i).start()
            if pair == 1:
                d2d(ph, z + NZ - s, s, c).start()
                d2d(ph, z + s, 3 + s, c).start()
        else:
            for i in (0, 1):
                zplus_in(ph, 4, i).wait_recv()
                zminus_in(ph, 4, i + 2).wait_recv()
            d2d(ph, z + 4, 7, c).start()

    def embed_ready(ph):
        for n in range(8):
            d2d(ph, z + d2d_z[n], n, 1 - c).wait_recv()

    def rows_of(j, yy):
        b, k = j // 4, j % 4
        if b == 0:
            return pl.ds(pl.multiple_of(256 + (yy % NY) * 128 + k * CHUNK, CHUNK), CHUNK)
        return pl.ds((b - 1) * 128 + k * CHUNK, CHUNK)

    right, left = dev(0, 1, 0, 1), dev(0, 3, 0, 1)

    def hx_own(j, s):
        r = rows_of(j, y)
        return rcopy(hid.at[r], hb.at[s, r], hx_s.at[s, j], hx_r.at[s, j], (right, left)[s])

    def hx_fwd(j):
        r = rows_of(j, y)
        s = 0 if j % 4 < 2 else 1
        return rcopy(hb.at[s, r], hb.at[1, r], hf_s.at[j], hx_r.at[1, j], (right, left)[s])

    def hx_in(j, s):
        r = rows_of(j, y)
        return rcopy(hb.at[s, r], hb.at[s, r], hf_s.at[j], hx_r.at[s, j], right)

    def yown(s, k, up):
        r = rows_of(k, y)
        if up:
            return rcopy(hb.at[s, r], hb.at[s, r], yp_s.at[s, k], yp_r.at[s, k], dev(0, 0, 1, 0))
        return rcopy(hb.at[s, r], hb.at[s, r], ym_s.at[s, k], ym_r.at[s, k], dev(0, 0, 3, 0))

    def yin(s, k, up):
        if up:
            r = rows_of(k, y + 3)
            return rcopy(hb.at[s, r], hb.at[s, r], yp_s.at[s, k], yp_r.at[s, k], dev(0, 0, 1, 0))
        r = rows_of(k, y + 1)
        return rcopy(hb.at[s, r], hb.at[s, r], ym_s.at[s, k], ym_r.at[s, k], dev(0, 0, 3, 0))

    def yfwd(s, k):
        if k < 2:
            r = rows_of(k, y + 3)
            return rcopy(hb.at[s, r], hb.at[s, r], yf_s.at[s, k], yf_r.at[s, k], dev(0, 0, 1, 0))
        r = rows_of(k, y + 1)
        return rcopy(hb.at[s, r], hb.at[s, r], yf_s.at[s, k], yf_r.at[s, k], dev(0, 0, 3, 0))

    def yfwd_in(s, k):
        r = rows_of(k, y + 2)
        return rcopy(hb.at[s, r], hb.at[s, r], yf_s.at[s, k], yf_r.at[s, k], dev(0, 0, 1, 0))

    def x_send(j):
        @pl.when(first)
        def _():
            hx_own(j, 0).start()
            hx_own(j, 1).start()

    def x_near(j):
        @pl.when(second)
        def _():
            for s in range(2):
                hx_in(j, s).wait_recv()
            if j < 4:
                hx_fwd(j).start()
                for s in range(2):
                    yown(s, j, True).start()
                    yown(s, j, False).start()

    def x_forward(*js):
        @pl.when(second)
        def _():
            for j in js:
                hx_fwd(j).start()

    def x_far(*js):
        @pl.when(first)
        def _():
            for j in js:
                hx_in(j, 1).wait_recv()
                if j < 4:
                    yown(1, j, True).start()
                    yown(1, j, False).start()

    def y_recv_of(s, k):
        yin(s, k, True).wait_recv()
        if k < 2:
            yfwd(s, k).start()
        yin(s, k, False).wait_recv()
        if k >= 2:
            yfwd(s, k).start()

    def y_near(k):
        @pl.when(second)
        def _():
            y_recv_of(1, k)
            y_recv_of(0, k)

    def y_far(k):
        @pl.when(first)
        def _():
            y_recv_of(1, k)

    def y_last(k):
        yfwd_in(1, k).wait_recv()

        @pl.when(second)
        def _():
            yfwd_in(0, k).wait_recv()

    my_owner = z // NY
    half = pl.ds(pl.multiple_of(c * 384, 384), 384)
    up, down = dev(1, 0, 0, 0), dev(NZ - 1, 0, 0, 0)

    def key_copy(o, n, to):
        return rcopy(kv.at[o, half], kv.at[o, half], kv_s.at[o, n], kv_r.at[o], to)

    def int_copy(o, n, to):
        return rcopy(om.at[o], om.at[o], om_s.at[o, n], om_r.at[o], to)

    def key_cross(o):
        return rcopy(kv.at[o, half], kv.at[o, half], kc_s.at[o], kc_r.at[o], dev(0, 0, 0, 1))

    def key_cross_in(o):
        ref = kv.at[o, pl.ds(pl.multiple_of(384 - c * 384, 384), 384)]
        return rcopy(ref, ref, kc_s.at[o], kc_r.at[o], dev(0, 0, 0, 1))

    def mt_send(n):
        to, s = ((dev(0, 2, 0, 0), 1), (right, 0), (left, 1))[n]
        return rcopy(om.at[2], mt.at[s], mt_s.at[n], mt_r.at[s], to)

    def small_sends():
        for cp in om_loads:
            cp.wait()

        @pl.when(first)
        def _():
            for n in range(3):
                mt_send(n).start()
            mt[0] = om[2]

    def key_sends():
        hid_load.wait()
        kp_load.wait()

        @pl.when(owner_here)
        def _():
            kv[my_owner, half, :] = jnp.dot(
                hb[own_slot, half, :], kp[...], preferred_element_type=F32
            ).astype(BF16)
            om[my_owner] = om[2]
            key_cross(my_owner).start()
            for n, to in enumerate((up, down)):
                key_copy(my_owner, n, to).start()
                int_copy(my_owner, n, to).start()

    def hops(o):
        return (z - y - NY * o + 2 * NZ) % NZ

    def key_relay(hop):
        for o in range(2):
            key_relay_of(o, hop)

    def key_relay_of(o, hop):
        @pl.when((hops(o) == hop) | ((hops(o) == NZ - hop) & (hop < 4)))
        def _():
            key_copy(o, 0, up).wait_recv()
            int_copy(o, 0, up).wait_recv()
            key_cross(o).start()

        if hop < 4:
            @pl.when(hops(o) == hop)
            def _():
                key_copy(o, 0, up).start()
                int_copy(o, 0, up).start()

        if hop < 3:
            @pl.when(hops(o) == NZ - hop)
            def _():
                key_copy(o, 1, down).start()
                int_copy(o, 1, down).start()

    def keys_sent(o):
        @pl.when(hops(o) < 4)
        def _():
            key_copy(o, 0, up).wait_send()
            int_copy(o, 0, up).wait_send()

        @pl.when((hops(o) > 5) | (hops(o) == 0))
        def _():
            key_copy(o, 1, down).wait_send()
            int_copy(o, 1, down).wait_send()

        key_cross(o).wait_send()

    def memory_ready():
        for o in range(2):
            key_cross_in(o).wait_recv()

        rcopy(om.at[2], mt.at[1], mt_s.at[0], mt_r.at[1], right).wait_recv()

        @pl.when(second)
        def _():
            rcopy(om.at[2], mt.at[0], mt_s.at[0], mt_r.at[0], right).wait_recv()

        lane = lax.broadcasted_iota(jnp.int32, (1, 128), 1)
        for s in range(2):
            live = lane < mt[s, 14:15, :]
            for o in range(2):
                owner_id = (y + NY * o) * NX + x
                named = live & (mt[s, 12:13, :] == owner_id)
                blocks = mt[s, 13:14, :].astype(F32)
                most = jnp.max(jnp.where(named, blocks, -1.0), axis=1, keepdims=True)
                least = jnp.min(jnp.where(named, blocks, 99.0), axis=1, keepdims=True)
                least = jnp.where(least == most, 99.0, least)
                mine = jnp.where(owner_id == z * NX + tok_x(s), 1.0, 0.0)
                for k, at_block in enumerate((most, least)):
                    n = 2 * o + k
                    keys = jnp.zeros((128, 128), F32)
                    tgts, docs = jnp.zeros((1, 128), F32), jnp.full((1, 128), -1.0, F32)
                    for b in range(6):
                        w = jnp.where(at_block == float(b), 1.0, 0.0)
                        keys = keys + w * kv[o, b * 128 : b * 128 + 128, :].astype(F32)
                        tgts = tgts + w * om[o, b : b + 1, :].astype(F32)
                        docs = docs + w * (om[o, 6 + b : 7 + b, :].astype(F32) + 1.0)
                    kg[s, n * 128 : n * 128 + 128, :] = keys.astype(BF16)
                    kt[s, n : n + 1, :] = tgts
                    kd[s, n : n + 1, :] = docs
                    ko[s, n : n + 1, :] = jnp.broadcast_to(mine * (at_block + 1.0) - 1.0, (1, 128))

    def column(s, row):
        return jnp.broadcast_to(mt[s, pl.ds(row, 1), :].astype(F32), (128, 128)).T

    def rows_at(blk):
        return pl.ds(pl.multiple_of(blk * 128, 128), 128)

    def two_blocks(sa, ba, sb, bb):
        return jnp.concatenate([hb[sa, rows_at(ba), :], hb[sb, rows_at(bb), :]], axis=0)

    def scores(sa, ba, sb, bb):
        qs = jnp.dot(two_blocks(sa, ba, sb, bb), kp[...], preferred_element_type=F32).astype(BF16)
        scores_of(sa, ba, rows_at(ba), qs[:128])
        scores_of(sb, bb, rows_at(bb), qs[128:])

    def scores_of(s, blk, r, q):
        tcol = column(s, blk)
        dcol = column(s, 6 + blk)
        i0 = lax.broadcasted_iota(jnp.int32, (128, 128), 0)
        i1 = lax.broadcasted_iota(jnp.int32, (128, 128), 1)
        eye = i0 == i1
        sc = SCALE * lax.dot_general(q, kg[s], (((1,), (1,)), ((), ())), preferred_element_type=F32)
        kept, hits = [], []
        for n in range(4):
            mine = jnp.where(ko[s, n : n + 1, :] == blk.astype(F32), 2.0, 0.0)
            keep = kd[s, n : n + 1, :] == dcol + jnp.where(eye, mine, 0.0)
            sk = jnp.where(keep, sc[:, n * 128 : n * 128 + 128], NEG)
            kept.append(sk)
            hits.append(jnp.where(kt[s, n : n + 1, :] == tcol, sk, NEG))

        def stats(tiles):
            top = tiles[0]
            for t in tiles[1:]:
                top = jnp.maximum(top, t)
            top = jnp.max(top, axis=1, keepdims=True)
            total = jnp.exp(tiles[0] - top)
            for t in tiles[1:]:
                total = total + jnp.exp(t - top)
            return top, jnp.sum(total, axis=1, keepdims=True)

        mp, mm = stats(kept)
        hp, hm = stats(hits)
        ms[s, r, :] = jnp.where(i1 == 4, mp, jnp.where(i1 == 5, mm, jnp.where(i1 == 6, hp, hm)))

    def logits(sa, ba, sb, bb, ph):
        a = two_blocks(sa, ba, sb, bb)
        for cs in range(2):
            res = jnp.dot(a, eb[ph, cs], preferred_element_type=F32)
            cols = slice(ph * 512 + cs * 256, ph * 512 + cs * 256 + 256)
            lg[sa, rows_at(ba), cols] = res[:128]
            lg[sb, rows_at(bb), cols] = res[128:]

    def finish(s, blk):
        r = pl.ds(pl.multiple_of(blk * 128, 128), 128)
        tcol = column(s, blk)
        i1 = lax.broadcasted_iota(jnp.int32, (128, 128), 1)
        lane = lax.broadcasted_iota(jnp.int32, (1, 128), 1)
        tiles = [lg[s, r, n * 128 : n * 128 + 128] for n in range(8)]
        top = tiles[0]
        for t in tiles[1:]:
            top = jnp.maximum(top, t)
        top = jnp.max(top, axis=1, keepdims=True)
        total, pick = None, None
        for n in range(8):
            ph, cs, half = n // 4, (n // 2) % 2, n % 2
            base = (2 * y + cs) * 2048 + x * 512 + ph * 256 + half * 128
            e = jnp.exp(tiles[n] - top)
            total = e if total is None else total + e
            h = jnp.where((lane + base).astype(F32) == tcol, tiles[n], NEG)
            pick = h if pick is None else jnp.maximum(pick, h)
        total = jnp.sum(total, axis=1, keepdims=True)
        pick = jnp.max(pick, axis=1, keepdims=True)
        tile = jnp.where(i1 == 0, top, jnp.where(i1 == 1, total, jnp.where(i1 == 2, pick, ms[s, r, :])))
        t = tile.T
        lp, lm, lh = t[0:1], t[1:2], t[2:3]
        mp, mm, hp, hm = t[4:5], t[5:6], t[6:7], t[7:8]
        peak = jnp.maximum(lp, mp)
        hit = jnp.maximum(lh, hp)
        st[s, 0, pl.ds(blk, 1), :] = peak
        st[s, 1, pl.ds(blk, 1), :] = lm * jnp.exp(lp - peak) + mm * jnp.exp(mp - peak)
        st[s, 2, pl.ds(blk, 1), :] = hit
        st[s, 3, pl.ds(blk, 1), :] = jnp.exp(lh - hit) + hm * jnp.exp(hp - hit)

    def finish2(sa, ba, sb, bb):
        finish(sa, ba)
        finish(sb, bb)

    for e in range(1, 4):
        xe(0, e).start()
    z_first(0, 0)
    z_first(1, 0)
    x_send(0)
    x_send(1)
    for e in range(1, 4):
        xe(1, e).start()
    small_sends()
    for j in range(2, 12):
        x_send(j)
    key_sends()
    z_first(0, 1)
    z_first(0, 2)

    z_events = [(ph, s, q) for ph in range(2) for s in range(1, 5) for q in range(2 if s < 4 else 1)]
    qy, qd, qu, qo = 2 + y, 2 + (y + 3) % 4, 2 + (y + 1) % 4, 2 + (y + 2) % 4
    plan = {}

    def at(u, fn, *args):
        plan.setdefault(u, []).append((fn, args))

    for n, ev in enumerate(z_events):
        at(n, z_event, *ev)
    at(4, z_first, 1, 1)
    at(5, z_first, 1, 2)
    for j, u in enumerate((0, 1, 3, 4, 6, 7, 8, 9, 10, 11, 12, 13)):
        at(u, x_near, j)
    for u, js in ((11, (4, 6)), (12, (5, 7)), (13, (8, 10)), (14, (9, 11))):
        at(u, x_forward, *js)
    for u, js in ((4, (0,)), (5, (1,)), (7, (2,)), (8, (3,)), (15, (4, 6)), (16, (5, 7)), (17, (8, 10)), (18, (9, 11))):
        at(u, x_far, *js)
    for k in range(4):
        at((6, 8, 10, 12)[k], y_near, k)
        at((9, 10, 11, 12)[k], y_far, k)
        at((15, 17, 16, 18)[k], y_last, k)
    for hop, u in ((1, 1), (2, 3), (3, 5), (4, 7)):
        at(u, key_relay, hop)
    groups = [
        [jnp.where(first, a, b) for a, b in zip(on_first, on_second)]
        for on_first, on_second in (
            ((0, 0, 0, 1), (0, qy, 1, qy)),
            ((0, qy, 0, qd), (0, 0, 1, 0)),
            ((0, qu, 0, qo), (0, qd, 1, qd)),
            ((1, qd, 1, qu), (0, qu, 1, qu)),
            ((1, qy, 1, 0), (0, 1, 1, 1)),
            ((1, 1, 1, qo), (0, qo, 1, qo)),
        )
    ]
    at(8, embed_ready, 0)
    at(9, memory_ready)
    for n, u in enumerate((8, 10, 12, 13)):
        at(u, logits, *groups[n], 0)
        at(max(u, 9), scores, *groups[n])
    at(14, embed_ready, 1)
    for n, u in enumerate((14, 14, 15, 15)):
        at(u, logits, *groups[n], 1)
        at(u, finish2, *groups[n])
    for n, u in ((4, 16), (5, 18)):
        at(u, logits, *groups[n], 0)
        at(u, logits, *groups[n], 1)
        at(u, scores, *groups[n])
        at(u, finish2, *groups[n])
    for u in range(22):
        for fn, args in plan.get(u, []):
            fn(*args)

    def r1_send(s):
        to, n = (left, 2) if s == 0 else (right, 3)
        return rcopy(st.at[s], r1.at[n], r1_s.at[s], r1_r.at[n], to)

    def r1_far():
        return rcopy(st.at[1], r1.at[1], r1_s.at[1], r1_r.at[1], dev(0, 2, 0, 0))

    def join(parts):
        peak, hit = parts[0][0], parts[0][2]
        for t in parts[1:]:
            peak = jnp.maximum(peak, t[0])
            hit = jnp.maximum(hit, t[2])
        mass, hmass = None, None
        for t in parts:
            m = t[1] * jnp.exp(t[0] - peak)
            h = t[3] * jnp.exp(t[2] - hit)
            mass = m if mass is None else mass + m
            hmass = h if hmass is None else hmass + h
        return peak, mass, hit, hmass

    def r2_send(n):
        return rcopy(st2, r2.at[y], r2_s.at[n], r2_r.at[y], (d, (v + n) % 8))

    @pl.when(second)
    def _():
        for s in range(2):
            r1_send(s).start()

    @pl.when(first)
    def _():
        r1_far().start()
        r1[0] = st[0]
        for n in range(1, 4):
            rcopy(st.at[0], r1.at[n], r1_s.at[0], r1_r.at[n], right).wait_recv()

        for i, t in enumerate(join([[r1[n, i] for i in range(4)] for n in range(4)])):
            st2[i] = t
        for n in range(1, 8):
            r2_send(n).start()
        r2[y] = st2[...]

    for n in range(4):
        @pl.when(jnp.logical_not(first & (y == n)))
        def _():
            rcopy(st2, r2.at[n], r2_s.at[0], r2_r.at[n], dev(0, 0, 0, 1)).wait_recv()

    peak, mass, hit, hmass = join([[r2[n, i] for i in range(4)] for n in range(4)])
    loss = peak + jnp.log(mass) - hit - jnp.log(hmass)
    out[...] = loss[0:6]

    for ph in range(2):
        for e in range(1, 4):
            xe(ph, e).wait_send()
        for s in range(1, 5):
            for i in range(4):
                if s < 4 or i < 2:
                    zplus(ph, s, i).wait_send()
                if s < 4 or i >= 2:
                    zminus(ph, s, i).wait_send()
        for n in range(8):
            d2d(ph, z + d2d_z[n], n, c).wait_send()

    for o in range(2):
        keys_sent(o)

    @pl.when(first)
    def _():
        for n in range(3):
            mt_send(n).wait_send()
        for j in range(12):
            for s in range(2):
                hx_own(j, s).wait_send()

    def y_sent(s):
        for k in range(4):
            yown(s, k, True).wait_send()
            yown(s, k, False).wait_send()
            yfwd(s, k).wait_send()

    y_sent(1)

    @pl.when(second)
    def _():
        for j in range(12):
            hx_fwd(j).wait_send()
        y_sent(0)
        for s in range(2):
            r1_send(s).wait_send()

    @pl.when(first)
    def _():
        r1_far().wait_send()
        for n in range(1, 8):
            r2_send(n).wait_send()


def per_device(hidden, out_embed, key_proj, targets, doc_ids, list_owner, list_block, list_count):
    dma = pltpu.SemaphoreType.DMA
    loss = pl.pallas_call(
        kernel,
        out_shape=jax.ShapeDtypeStruct((6, 128), F32),
        in_specs=[pl.BlockSpec(memory_space=pltpu.HBM)] * 5 + [pl.BlockSpec(memory_space=pltpu.VMEM)] * 2 + [pl.BlockSpec(memory_space=pltpu.SMEM)],
        out_specs=pl.BlockSpec(memory_space=pltpu.VMEM),
        scratch_shapes=[
            pltpu.VMEM((3, 768, 4096), BF16),
            pltpu.VMEM((2, 2, 4096, 256), BF16),
            pltpu.VMEM((4096, 128), BF16),
            pltpu.VMEM((2, 768, 1024), F32),
            pltpu.VMEM((2, 768, 128), BF16),
            pltpu.VMEM((2, 16, 128), jnp.int32),
            pltpu.VMEM((3, 16, 128), jnp.int32),
            pltpu.VMEM((2, 512, 128), BF16),
            pltpu.VMEM((2, 8, 128), F32),
            pltpu.VMEM((2, 8, 128), F32),
            pltpu.VMEM((2, 8, 128), F32),
            pltpu.VMEM((2, 768, 128), F32),
            pltpu.VMEM((2, 4, 8, 128), F32),
            pltpu.VMEM((4, 4, 8, 128), F32),
            pltpu.VMEM((4, 8, 128), F32),
            pltpu.VMEM((4, 4, 8, 128), F32),
            dma((5,)),
            dma((2, 4)), dma((2, 4)),
            dma((2, 4, 4)), dma((2, 4, 4)), dma((2, 4, 4)), dma((2, 4, 4)),
            dma((2, 8)), dma((2, 8)),
            dma((2, 12)), dma((12,)), dma((2, 12)),
            dma((2, 4)), dma((2, 4)), dma((2, 4)), dma((2, 4)), dma((2, 4)), dma((2, 4)),
            dma((2, 2)), dma((2,)), dma((2, 2)), dma((2,)), dma((2,)), dma((2,)), dma((4,)), dma((2,)),
            dma((2,)), dma((4,)), dma((8,)), dma((4,)),
        ],
        compiler_params=pltpu.CompilerParams(
            collective_id=0, has_side_effects=True, vmem_limit_bytes=56 * 2**20
        ),
    )(hidden, out_embed, key_proj, targets, doc_ids, list_owner, list_block, list_count)
    return loss.reshape(768)


def solution(mesh):
    placed = (
        P("dp", None),
        P("dp", "vocab"),
        P(),
        P("dp"),
        P("dp"),
        P("dp", None),
        P("dp", None),
        P("dp"),
    )
    return jax.shard_map(per_device, mesh=mesh, in_specs=placed, out_specs=P("dp"), check_vma=False)
```

time: 302 us -> 89.3 us (0.30)
  waiting for transfers between devices: 142 us -> 0 us
  blocking collectives: 102 us -> 0 us
  Pallas kernels: 0 us -> 87.2 us
  matrix products: 28.1 us -> 0 us
  between operations: 14.2 us -> 0.66 us
  other arithmetic: 7.3 us -> 0 us
  local copies, waits for them, and re-layouts: 7.27 us -> 1.28 us
    all_gather x2 -> x0, waiting for transfers between devices: 142 us -> none  [the longest x1 127 us: per_device(): lax.all_gather(out_embed, 'dp', axis=0, tiled=True)]
    pallas_call x0 -> x1, Pallas kernels: none -> 87.2 us  [per_device(): pl.pallas_call(kernel, out_shape=jax.ShapeDtypeStruct((6, 128), F32), in_...]
    all_gather x2 -> x0, blocking collectives: 75 us -> none  [the longest x1 39.3 us: per_device(): lax.all_gather(doc_ids, 'dp', axis=0, tiled=True)]
    dot_general x3 -> x0, matrix products: 28.1 us -> none  [the longest x1 18.3 us: per_device(): jnp.dot(hidden, lax.all_gather(out_embed, 'dp', axis=0, tiled=True), pref...]
    psum x1 -> x0, blocking collectives: 14.5 us -> none  [per_device(): lax.psum((mass_value * jnp.exp(peak_value - top_peak), hit_mass * jnp.exp...]
    pmax x1 -> x0, blocking collectives: 13 us -> none  [per_device(): top_peak, top_hit = lax.pmax((peak_value, hit_peak), 'vocab')]
    reduce_sum x2 -> x0, other arithmetic: 6.57 us -> none  [the longest x1 3.85 us: masked_stats(): jnp.sum(jnp.exp(jnp.where(keep_mask, values - peak_value[:, None], negati...]
    gather x3 -> x0, local copies, waits for them, and re-layouts: 4.93 us -> none  [the longest x1 3.73 us: per_device(): every_key.reshape(-1, KB, key_width)[slot_ids].reshape(-1, key_width)]
  transfers between devices with their start and end apart: 2 -> 0, of which waited for: 2 -> 0; matrix products, arithmetic and copies ran while one was open for 5% -> 0% of each run, Pallas kernels for 0% -> 0%
where the time goes in v1:
time: 89.3 us; the launch traced here: 89.1 us
  Pallas kernels  87.2 us (98%)
  local copies, waits for them, and re-layouts  1.28 us (1%)
    pallas_call x1, Pallas kernels, per_device(): pl.pallas_call(kernel, out_shape=jax.ShapeDtypeStruct((6, 128), F32), in_...  87.2 us

profile of v1, /device:TPU:1, one launch (start us, length us, event | category | flops | bytes accessed | tf_op | source)
XLA Modules:
  0.0 89.1 jit_solution(5750191362395350156)
XLA Ops:
  0.7 87.2 %shard_map.82 = f32[6,128]{1,0:T(8,128)} custom-call(bf16[768,4096]{1,0:T(8,128)(2,1)} %hid.1, bf16[128,2048]{1,0:T(8,128)(2,1)} %emb.1, bf16[4096,128]{1,0:T(8,128)(2,1)} %kproj.1, s32[768]{0:T(1024)} %tgt.1, s32[768]{0:T(1024)} %doc.1, s32[1,64]{1,0:T(1,128)} %lown.1, s32[1,64]{1,0:T(1,128)} %lblk.1, s32[1]{0:T(128)S(6)} %copy.10.lcnt), custom_call_target="tpu_custom_call" | custom-call | tf_op jit(solution)/shard_map/pallas_call | solution.py:621
  87.9 1.3 %copy.11 = f32[768]{0:T(1024)} copy(f32[768]{0:T(1024)} %bitcast.1) | data formatting | bytes 6144

commit v2 on v1

v2 whole, which is shorter than its diff:
```python
import jax
import jax.numpy as jnp
from jax import lax
from jax.experimental import pallas as pl
from jax.experimental.pallas import tpu as pltpu
from jax.sharding import PartitionSpec as P

MESH = pl.DeviceIdType.MESH
NEG = -1e30
SCALE = 3.0 / 128**0.5
NX, NY, NZ = 4, 4, 8
CHUNK = 32
F32 = jnp.float32
WIDTH, OFFSET = (256, 256), (0, 256)
BF16 = jnp.bfloat16


def kernel(
    hid, emb, kproj, tgt, doc, lown, lblk, lcnt, out,
    hb, eb0, eb1, kp, kv, mt, om, kg, kt, kd, ko, tc, dc, sp, sm, st, last, rr, rl,
    loc_sem, xe_s, xe_r, z_s, z_r, dc_s, dc_r,
    hx_s, hf_s, hx_r, y_s, y_r, yf_r,
    kv_s, kv_r, om_s, om_r, kc_s, kc_r, mt_s, mt_r, r_s, r_r, rl_s, rl_r,
):
    d = lax.axis_index("dp")
    v = lax.axis_index("vocab")
    z, x = d // NX, d % NX
    y, c = v // 2, v % 2
    owner_here = z % NY == y
    first, second = c == 0, c == 1

    def eb(ph, row, rows, shard):
        w = WIDTH[ph]
        return (eb0, eb1)[ph].at[pl.ds(row, rows), pl.ds(pl.multiple_of(shard * w, 128), w)]

    def tok_x(s):
        return (x + 3 * c + 2 * s) % NX

    def dev(dz, dx, dy, dc):
        return (((z + dz) % NZ) * NX + (x + dx) % NX, ((y + dy) % NY) * 2 + (c + dc) % 2)

    def rcopy(src, dst, ssem, rsem, to):
        return pltpu.make_async_remote_copy(
            src_ref=src, dst_ref=dst, send_sem=ssem, recv_sem=rsem, device_id=to, device_id_type=MESH
        )

    bar = pltpu.get_barrier_semaphore()
    for to in [dev(1, 0, 0, 0), dev(NZ - 1, 0, 0, 0)] + [
        dev(0, 1, 0, 0), dev(0, 2, 0, 0), dev(0, 3, 0, 0), dev(0, 1, 0, 1), dev(0, 3, 0, 1)
    ]:
        pl.semaphore_signal(bar, inc=1, device_id=to, device_id_type=MESH)
    for n in range(1, 8):
        pl.semaphore_signal(bar, inc=1, device_id=(d, (v + n) % 8), device_id_type=MESH)

    om_loads = []
    for n in range(6):
        om_loads.append(pltpu.make_async_copy(tgt.at[pl.ds(n * 128, 128)], om.at[2, n], loc_sem.at[4]))
        om_loads.append(pltpu.make_async_copy(doc.at[pl.ds(n * 128, 128)], om.at[2, 6 + n], loc_sem.at[4]))
    for cp in om_loads:
        cp.start()
    emb_loads = []
    for ph in range(2):
        col = pl.multiple_of(x * 512 + OFFSET[ph], 128)
        cp = pltpu.make_async_copy(
            emb.at[:, pl.ds(col, WIDTH[ph])], eb(ph, pl.multiple_of(d * 128, 128), 128, c), loc_sem.at[2 + ph]
        )
        cp.start()
        emb_loads.append(cp)
    own_slot = 2 * c
    kp_load = pltpu.make_async_copy(kproj, kp, loc_sem.at[1])
    kp_load.start()
    hid_load = pltpu.make_async_copy(hid, hb.at[own_slot], loc_sem.at[0])
    hid_load.start()
    om[2, 12:16] = jnp.zeros((4, 128), jnp.int32)
    om[2, 12:13, 0:64] = lown[...]
    om[2, 13:14, 0:64] = lblk[...]
    om[2, 14:15] = jnp.full((1, 128), lcnt[0], jnp.int32)
    pl.semaphore_wait(bar, 14)

    def eslot(ph, zz, i):
        row = ((zz % NZ) * NX + (x + i) % NX) * 128
        return eb(ph, pl.multiple_of(row, 128), 128, c)

    def xe(ph, e):
        col = pl.multiple_of(((x + e) % NX) * 512 + OFFSET[ph], 128)
        return rcopy(
            emb.at[:, pl.ds(col, WIDTH[ph])],
            eb(ph, pl.multiple_of(d * 128, 128), 128, c),
            xe_s.at[0], xe_r.at[ph, 4 - e], dev(0, e, 0, 0),
        )

    def xe_in(ph, i):
        return rcopy(
            emb.at[:, pl.ds(0, WIDTH[ph])], eslot(ph, z, i), xe_s.at[0], xe_r.at[ph, i], dev(0, i, 0, 0)
        )

    def zplus(ph, s, i):
        ref = eslot(ph, z - (s - 1) + NZ, i)
        return rcopy(ref, ref, z_s.at[0], z_r.at[ph, s - 1, i], dev(1, 0, 0, 0))

    def zminus(ph, s, i):
        ref = eslot(ph, z + (s - 1), i)
        return rcopy(ref, ref, z_s.at[0], z_r.at[ph, s - 1, i - 2 if s == 4 else i], dev(NZ - 1, 0, 0, 0))

    def z_in(ph, s, i):
        ref = eb(ph, 0, 256, c)
        return rcopy(ref, ref, z_s.at[0], z_r.at[ph, s - 1, i], dev(1, 0, 0, 0))

    def d2d(ph, zz, n, shard):
        ref = eb(ph, pl.multiple_of((zz % NZ) * 512, 512), 512, shard)
        return rcopy(ref, ref, dc_s.at[0], dc_r.at[ph], dev(0, 0, 0, 1))

    d2d_z = [0, 7, 6, 5, 1, 2, 3, 4]

    def z_first(ph, pair):
        for i in ((0,), (1,), (2, 3))[pair]:
            if i == 0:
                emb_loads[ph].wait()
            else:
                xe_in(ph, i).wait_recv()
            zplus(ph, 1, i).start()
            zminus(ph, 1, i).start()
        if pair == 2:
            d2d(ph, z, 0, c).start()

    def z_event(ph, s, pair):
        if s < 4:
            for i in (0, 1) if pair == 0 else (2, 3):
                z_in(ph, s, i).wait_recv()
                if s < 3 or i < 2:
                    zplus(ph, s + 1, i).start()
                if s < 3 or i >= 2:
                    zminus(ph, s + 1, i).start()
            if pair == 1:
                d2d(ph, z + NZ - s, s, c).start()
                d2d(ph, z + s, 3 + s, c).start()
        else:
            for i in (0, 1):
                z_in(ph, 4, i).wait_recv()
            d2d(ph, z + 4, 7, c).start()

    def embed_ready(ph):
        ref = eb(ph, 0, 4096, 1 - c)
        rcopy(ref, ref, dc_s.at[0], dc_r.at[ph], dev(0, 0, 0, 1)).wait_recv()

    def rows_of(j, yy):
        b, k = j // 4, j % 4
        if b == 0:
            return pl.ds(pl.multiple_of(256 + (yy % NY) * 128 + k * CHUNK, CHUNK), CHUNK)
        return pl.ds((b - 1) * 128 + k * CHUNK, CHUNK)

    right, left = dev(0, 1, 0, 1), dev(0, 3, 0, 1)

    def hx_own(j, s):
        r = rows_of(j, y)
        return rcopy(hid.at[r], hb.at[s, r], hx_s.at[0], hx_r.at[j], (right, left)[s])

    def hx_fwd(j):
        r = rows_of(j, y)
        s = 0 if j % 4 < 2 else 1
        return rcopy(hb.at[s, r], hb.at[1, r], hf_s.at[0], hx_r.at[j], (right, left)[s])

    def arrived(sem, rows):
        ref = hb.at[0, pl.ds(0, rows)]
        rcopy(ref, ref, hf_s.at[0], sem, right).wait_recv()

    def yown(s, k, up):
        r = rows_of(k, y)
        if up:
            return rcopy(hb.at[s, r], hb.at[s, r], y_s.at[0], y_r.at[k], dev(0, 0, 1, 0))
        return rcopy(hb.at[s, r], hb.at[s, r], y_s.at[0], y_r.at[k], dev(0, 0, 3, 0))

    def yfwd(s, k):
        if k < 2:
            r = rows_of(k, y + 3)
            return rcopy(hb.at[s, r], hb.at[s, r], y_s.at[0], yf_r.at[k], dev(0, 0, 1, 0))
        r = rows_of(k, y + 1)
        return rcopy(hb.at[s, r], hb.at[s, r], y_s.at[0], yf_r.at[k], dev(0, 0, 3, 0))

    def x_send(j):
        @pl.when(first)
        def _():
            hx_own(j, 0).start()
            hx_own(j, 1).start()

    def x_near(j):
        @pl.when(second)
        def _():
            arrived(hx_r.at[j], 64)
            if j < 4:
                hx_fwd(j).start()
                for s in range(2):
                    yown(s, j, True).start()
                    yown(s, j, False).start()

    def x_forward(*js):
        @pl.when(second)
        def _():
            for j in js:
                hx_fwd(j).start()

    def x_far(*js):
        @pl.when(first)
        def _():
            for j in js:
                arrived(hx_r.at[j], 32)
                if j < 4:
                    yown(1, j, True).start()
                    yown(1, j, False).start()

    def y_near(k):
        @pl.when(second)
        def _():
            arrived(y_r.at[k], 128)
            yfwd(0, k).start()
            yfwd(1, k).start()

    def y_far(k):
        @pl.when(first)
        def _():
            arrived(y_r.at[k], 64)
            yfwd(1, k).start()

    def y_last(k):
        @pl.when(first)
        def _():
            arrived(yf_r.at[k], 32)

        @pl.when(second)
        def _():
            arrived(yf_r.at[k], 64)

    my_owner = z // NY
    half = pl.ds(pl.multiple_of(c * 384, 384), 384)
    up, down = dev(1, 0, 0, 0), dev(NZ - 1, 0, 0, 0)

    def key_copy(o, n, to):
        return rcopy(kv.at[o, half], kv.at[o, half], kv_s.at[o], kv_r.at[o], to)

    def int_copy(o, n, to):
        return rcopy(om.at[o], om.at[o], om_s.at[o], om_r.at[o], to)

    def key_cross(o):
        return rcopy(kv.at[o, half], kv.at[o, half], kc_s.at[0], kc_r.at[o], dev(0, 0, 0, 1))

    def key_cross_in(o):
        ref = kv.at[o, pl.ds(pl.multiple_of(384 - c * 384, 384), 384)]
        return rcopy(ref, ref, kc_s.at[0], kc_r.at[o], dev(0, 0, 0, 1))

    def mt_send(n):
        to, s = ((dev(0, 2, 0, 0), 1), (right, 0), (left, 1))[n]
        return rcopy(om.at[2], mt.at[s], mt_s.at[0], mt_r.at[s], to)

    def small_sends():
        for cp in om_loads:
            cp.wait()

        @pl.when(first)
        def _():
            for n in range(3):
                mt_send(n).start()
            mt[0] = om[2]

    def key_sends():
        hid_load.wait()
        kp_load.wait()

        @pl.when(owner_here)
        def _():
            kv[my_owner, half, :] = jnp.dot(
                hb[own_slot, half, :], kp[...], preferred_element_type=F32
            ).astype(BF16)
            om[my_owner] = om[2]
            key_cross(my_owner).start()
            for n, to in enumerate((up, down)):
                key_copy(my_owner, n, to).start()
                int_copy(my_owner, n, to).start()

    def hops(o):
        return (z - y - NY * o + 2 * NZ) % NZ

    def key_relay(hop):
        for o in range(2):
            key_relay_of(o, hop)

    def key_relay_of(o, hop):
        @pl.when((hops(o) == hop) | ((hops(o) == NZ - hop) & (hop < 4)))
        def _():
            key_copy(o, 0, up).wait_recv()
            int_copy(o, 0, up).wait_recv()
            key_cross(o).start()

        if hop < 4:
            @pl.when(hops(o) == hop)
            def _():
                key_copy(o, 0, up).start()
                int_copy(o, 0, up).start()

        if hop < 3:
            @pl.when(hops(o) == NZ - hop)
            def _():
                key_copy(o, 1, down).start()
                int_copy(o, 1, down).start()

    def keys_sent(o):
        def sent(ref, sem):
            rcopy(ref, ref, sem, kv_r.at[o], up).wait_send()

        @pl.when(hops(o) == 0)
        def _():
            sent(kv.at[o], kv_s.at[o])
            sent(om.at[0:2], om_s.at[o])

        @pl.when(((hops(o) > 0) & (hops(o) < 4)) | (hops(o) > 5))
        def _():
            sent(kv.at[o, half], kv_s.at[o])
            sent(om.at[o], om_s.at[o])

    def keys_ready():
        for o in range(2):
            key_cross_in(o).wait_recv()

    def tokens_ready():
        rcopy(om.at[2], mt.at[1], mt_s.at[0], mt_r.at[1], right).wait_recv()

        @pl.when(second)
        def _():
            rcopy(om.at[2], mt.at[0], mt_s.at[0], mt_r.at[0], right).wait_recv()

        def turn(blk, _):
            for s in range(2):
                tc[s, blk] = column(s, blk)
                dc[s, blk] = column(s, 6 + blk)
            return 0

        lax.fori_loop(0, 6, turn, 0)

    def memory_ready():
        keys_ready()
        lane = lax.broadcasted_iota(jnp.int32, (1, 128), 1)
        for s in range(2):
            live = lane < mt[s, 14:15, :]
            for o in range(2):
                owner_id = (y + NY * o) * NX + x
                named = live & (mt[s, 12:13, :] == owner_id)
                blocks = mt[s, 13:14, :].astype(F32)
                most = jnp.max(jnp.where(named, blocks, -1.0), axis=1, keepdims=True)
                least = jnp.min(jnp.where(named, blocks, 99.0), axis=1, keepdims=True)
                least = jnp.where(least == most, 99.0, least)
                mine = jnp.where(owner_id == z * NX + tok_x(s), 1.0, 0.0)
                for k, at_block in enumerate((most, least)):
                    n = 2 * o + k
                    keys = jnp.zeros((128, 128), F32)
                    tgts, docs = jnp.zeros((1, 128), F32), jnp.full((1, 128), -1.0, F32)
                    for b in range(6):
                        w = jnp.where(at_block == float(b), 1.0, 0.0)
                        keys = keys + w * kv[o, b * 128 : b * 128 + 128, :].astype(F32)
                        tgts = tgts + w * om[o, b : b + 1, :].astype(F32)
                        docs = docs + w * (om[o, 6 + b : 7 + b, :].astype(F32) + 1.0)
                    kg[s, n * 128 : n * 128 + 128, :] = keys.astype(BF16)
                    kt[s, n : n + 1, :] = tgts
                    kd[s, n : n + 1, :] = docs
                    ko[s, n : n + 1, :] = jnp.broadcast_to(mine * (at_block + 1.0) - 1.0, (1, 128))

    def column(s, row):
        return jnp.broadcast_to(mt[s, pl.ds(row, 1), :].astype(F32), (128, 128)).T

    def rows_at(blk):
        return pl.ds(pl.multiple_of(blk * 128, 128), 128)

    def two_blocks(sa, ba, sb, bb):
        return jnp.concatenate([hb[sa, rows_at(ba), :], hb[sb, rows_at(bb), :]], axis=0)

    def peaks(tiles):
        top = tiles[0]
        for t in tiles[1:]:
            top = jnp.maximum(top, t)
        top = jnp.max(top, axis=1, keepdims=True)
        total = jnp.exp(tiles[0] - top)
        for t in tiles[1:]:
            total = total + jnp.exp(t - top)
        return top, jnp.sum(total, axis=1, keepdims=True)

    def halves(n):
        sa, ba, sb, bb = groups[n]
        return (0, sa, ba), (1, sb, bb)

    def lane_tile(first_lane, columns):
        i1 = lax.broadcasted_iota(jnp.int32, (128, 128), 1)
        t = columns[-1]
        for k in range(len(columns) - 2, -1, -1):
            t = jnp.where(i1 == first_lane + k, columns[k], t)
        return t

    def score_tiles(n):
        q2 = jnp.dot(two_blocks(*groups[n]), kp[...], preferred_element_type=F32).astype(BF16)
        i0 = lax.broadcasted_iota(jnp.int32, (128, 128), 0)
        i1 = lax.broadcasted_iota(jnp.int32, (128, 128), 1)
        eye = i0 == i1
        out_tiles = []
        for h, s, blk in halves(n):
            q = q2[h * 128 : h * 128 + 128]
            tcol, dcol = tc[s, blk], dc[s, blk]
            sc = SCALE * lax.dot_general(q, kg[s], (((1,), (1,)), ((), ())), preferred_element_type=F32)
            kept, hits = [], []
            for m in range(4):
                mine = jnp.where(ko[s, m : m + 1, :] == blk.astype(F32), 2.0, 0.0)
                keep = kd[s, m : m + 1, :] == dcol + jnp.where(eye, mine, 0.0)
                sk = jnp.where(keep, sc[:, m * 128 : m * 128 + 128], NEG)
                kept.append(sk)
                hits.append(jnp.where(kt[s, m : m + 1, :] == tcol, sk, NEG))
            out_tiles.append(lane_tile(4, [*peaks(kept), *peaks(hits)]))
        return out_tiles

    def logit_columns(n, phs):
        a = two_blocks(*groups[n])
        lane = lax.broadcasted_iota(jnp.int32, (1, 128), 1)
        res = [
            (ph, cs, jnp.dot(a, (eb0, eb1)[ph][:, cs * 256 : cs * 256 + 256], preferred_element_type=F32))
            for ph in phs
            for cs in range(2)
        ]
        out_columns = []
        for h, s, blk in halves(n):
            tcol = tc[s, blk]
            tiles, pick = [], None
            for ph, cs, r in res:
                for k in range(2):
                    t = r[h * 128 : h * 128 + 128, k * 128 : k * 128 + 128]
                    base = (2 * y + cs) * 2048 + x * 512 + OFFSET[ph] + k * 128
                    hit = jnp.where((lane + base).astype(F32) == tcol, t, NEG)
                    pick = hit if pick is None else jnp.maximum(pick, hit)
                    tiles.append(t)
            out_columns.append([*peaks(tiles), jnp.max(pick, axis=1, keepdims=True)])
        return out_columns

    def early(n):
        columns = logit_columns(n, (0,))
        memory = score_tiles(n)
        for h in range(2):
            sp[n, h] = lane_tile(8, columns[h])
            sm[n, h] = memory[h]

    def late(was_early, *ns):
        rows = [r for n in ns for r in late_rows(n, was_early)]
        for n, h, s, blk, values in rows:
            for k, row in enumerate(values):
                if n < 5:
                    st[s, k, pl.ds(blk, 1), :] = row
                else:
                    last[s, pl.ds(k + (4 * (1 - c) if h else 0), 1), :] = row

    def late_rows(n, was_early):
        i1 = lax.broadcasted_iota(jnp.int32, (128, 128), 1)
        columns = logit_columns(n, (1,) if was_early else (0, 1))
        memory = [sm[n, 0], sm[n, 1]] if was_early else score_tiles(n)
        rows = []
        for h, s, blk in halves(n):
            t = jnp.where(i1 < 4, lane_tile(0, columns[h]), memory[h])
            if was_early:
                t = jnp.where(i1 < 8, t, sp[n, h])
            t = t.T
            parts = [(t[0:1], t[1:2], t[2:3], 1.0), (t[4:5], t[5:6], t[6:7], t[7:8])]
            if was_early:
                parts.append((t[8:9], t[9:10], t[10:11], 1.0))
            peak, hit = parts[0][0], parts[0][2]
            for lp, _, lh, _ in parts[1:]:
                peak, hit = jnp.maximum(peak, lp), jnp.maximum(hit, lh)
            mass, hmass = None, None
            for lp, lm, lh, hm in parts:
                m, g = lm * jnp.exp(lp - peak), hm * jnp.exp(lh - hit)
                mass = m if mass is None else mass + m
                hmass = g if hmass is None else hmass + g
            rows.append((n, h, s, blk, (peak, mass, hit, hmass)))
        return rows

    def st_send(s, n):
        to = (z * NX + tok_x(s), (v + n) % 8)
        return rcopy(st.at[s], rr.at[(2 * c + s) * NY + y], r_s.at[0], r_r.at[0], to)

    def last_send(s, n):
        to = (z * NX + tok_x(s), (v + n) % 8)
        return rcopy(last.at[s], rl.at[(2 * c + s) * NY + y - 4], rl_s.at[0], rl_r.at[0], to)

    def most_results():
        for n in range(1, 8):
            for s in range(2):
                st_send(s, n).start()
        st_send(1, 0).start()

        @pl.when(second)
        def _():
            st_send(0, 0).start()

        @pl.when(first)
        def _():
            rr[y] = st[0]

    for e in range(1, 4):
        xe(0, e).start()
    z_first(0, 0)
    z_first(1, 0)
    x_send(0)
    x_send(1)
    for e in range(1, 4):
        xe(1, e).start()
    small_sends()
    for j in range(2, 12):
        x_send(j)
    key_sends()
    z_first(0, 1)
    z_first(0, 2)

    z_events = [(ph, s, q) for ph in range(2) for s in range(1, 5) for q in range(2 if s < 4 else 1)]
    qy, qd, qu, qo = 2 + y, 2 + (y + 3) % 4, 2 + (y + 1) % 4, 2 + (y + 2) % 4
    plan = {}

    def at(u, fn, *args):
        plan.setdefault(u, []).append((fn, args))

    for n, ev in enumerate(z_events):
        at(n, z_event, *ev)
    for hop, u in ((1, 0), (2, 2), (3, 4), (4, 5)):
        at(u, key_relay, hop)
    at(3, z_first, 1, 1)
    at(4, z_first, 1, 2)
    for j, u in enumerate((-1, 1, 4, 5, 7, 8, 9, 10, 11, 12, 14, 14)):
        at(u, x_near, j)
    for u, js in ((11, (4, 6)), (12, (5, 7)), (14, (8, 10)), (14, (9, 11))):
        at(u, x_forward, *js)
    for u, js in ((4, (0,)), (5, (1,)), (7, (2,)), (8, (3,)), (15, (4, 6)), (16, (5, 7)), (17, (8, 10)), (18, (9, 11))):
        at(u, x_far, *js)
    for k in range(4):
        at((6, 8, 10, 12)[k], y_near, k)
        at((10, 11, 13, 14)[k], y_far, k)
        at((15, 17, 16, 18)[k], y_last, k)
    groups = [
        [jnp.where(first, a, b) for a, b in zip(on_first, on_second)]
        for on_first, on_second in (
            ((0, 0, 0, 1), (0, qy, 1, qy)),
            ((0, qy, 0, qd), (0, 0, 1, 0)),
            ((0, qu, 0, qo), (0, qd, 1, qd)),
            ((1, qd, 1, qu), (0, qu, 1, qu)),
            ((1, qy, 1, 0), (0, 1, 1, 1)),
            ((1, 1, 1, qo), (0, qo, 1, qo)),
        )
    ]
    at(4, tokens_ready)
    at(7, memory_ready)
    at(8, embed_ready, 0)
    at(8, early, 0)
    at(10, early, 1)
    at(12, early, 2)
    at(14, early, 3)
    at(14, embed_ready, 1)
    at(14, late, True, 0, 1)
    at(14, late, True, 2, 3)
    at(16, late, False, 4)
    at(18, late, False, 5)
    at(17, most_results)
    for u in range(-1, 22):
        for fn, args in plan.get(u, []):
            fn(*args)

    for n in range(8):
        last_send(1, n).start()

    @pl.when(second)
    def _():
        for n in range(8):
            last_send(0, n).start()

    @pl.when(first)
    def _():
        rcopy(rr.at[0:15], rr.at[0:15], r_s.at[0], r_r.at[0], right).wait_recv()

    @pl.when(second)
    def _():
        rcopy(rr, rr, r_s.at[0], r_r.at[0], right).wait_recv()

    rcopy(rl, rl, rl_s.at[0], rl_r.at[0], right).wait_recv()
    for n in range(4):
        far_blk = 2 + (n + 2) % 4
        for k in range(4):
            rr[4 + n, k, 1:2] = rl[n, k : k + 1]
            rr[4 + n, k, far_blk : far_blk + 1] = rl[n, 4 + k : 5 + k]
            for m in (4, 8):
                rr[4 + m + n, k, far_blk : far_blk + 1] = rl[m + n, k : k + 1]

    peak, hit = rr[0, 0], rr[0, 2]
    for n in range(1, 16):
        peak = jnp.maximum(peak, rr[n, 0])
        hit = jnp.maximum(hit, rr[n, 2])
    mass = rr[0, 1] * jnp.exp(rr[0, 0] - peak)
    hmass = rr[0, 3] * jnp.exp(rr[0, 2] - hit)
    for n in range(1, 16):
        mass = mass + rr[n, 1] * jnp.exp(rr[n, 0] - peak)
        hmass = hmass + rr[n, 3] * jnp.exp(rr[n, 2] - hit)
    loss = peak + jnp.log(mass) - hit - jnp.log(hmass)
    out[...] = loss[0:6]

    def sent(ref, sem):
        rcopy(ref, ref, sem.at[0], dc_r.at[0], right).wait_send()

    sent(hb.at[0, pl.ds(0, 48)], xe_s)
    sent(hb.at[0, pl.ds(0, 448)], z_s)
    sent(hb.at[0, pl.ds(0, 512)], dc_s)
    sent(kv.at[0], kc_s)
    for o in range(2):
        keys_sent(o)

    @pl.when(first)
    def _():
        sent(om, mt_s)
        sent(hb.at[0], hx_s)
        sent(hb.at[0, pl.ds(0, 384)], y_s)
        sent(rr.at[0:15], r_s)
        sent(rl.at[0:8], rl_s)

    @pl.when(second)
    def _():
        sent(hb.at[0, pl.ds(0, 384)], hf_s)
        sent(hb.at[0], y_s)
        sent(rr, r_s)
        sent(tc.at[0, 0:1], rl_s)


def per_device(hidden, out_embed, key_proj, targets, doc_ids, list_owner, list_block, list_count):
    dma = pltpu.SemaphoreType.DMA
    loss = pl.pallas_call(
        kernel,
        out_shape=jax.ShapeDtypeStruct((6, 128), F32),
        in_specs=[pl.BlockSpec(memory_space=pltpu.HBM)] * 5 + [pl.BlockSpec(memory_space=pltpu.VMEM)] * 2 + [pl.BlockSpec(memory_space=pltpu.SMEM)],
        out_specs=pl.BlockSpec(memory_space=pltpu.VMEM),
        scratch_shapes=[
            pltpu.VMEM((3, 768, 4096), BF16),
            pltpu.VMEM((4096, 512), BF16),
            pltpu.VMEM((4096, 512), BF16),
            pltpu.VMEM((4096, 128), BF16),
            pltpu.VMEM((2, 768, 128), BF16),
            pltpu.VMEM((2, 16, 128), jnp.int32),
            pltpu.VMEM((3, 16, 128), jnp.int32),
            pltpu.VMEM((2, 512, 128), BF16),
            pltpu.VMEM((2, 8, 128), F32),
            pltpu.VMEM((2, 8, 128), F32),
            pltpu.VMEM((2, 8, 128), F32),
            pltpu.VMEM((2, 6, 128, 128), F32),
            pltpu.VMEM((2, 6, 128, 128), F32),
            pltpu.VMEM((4, 2, 128, 128), F32),
            pltpu.VMEM((4, 2, 128, 128), F32),
            pltpu.VMEM((2, 4, 8, 128), F32),
            pltpu.VMEM((2, 8, 128), F32),
            pltpu.VMEM((16, 4, 8, 128), F32),
            pltpu.VMEM((12, 8, 128), F32),
            dma((5,)),
            dma((1,)), dma((2, 4)), dma((1,)), dma((2, 4, 4)), dma((1,)), dma((2,)),
            dma((1,)), dma((1,)), dma((12,)), dma((1,)), dma((4,)), dma((4,)),
            dma((2,)), dma((2,)), dma((2,)), dma((2,)), dma((1,)), dma((2,)), dma((1,)), dma((2,)),
            dma((1,)), dma((1,)), dma((1,)), dma((1,)),
        ],
        compiler_params=pltpu.CompilerParams(
            collective_id=0, has_side_effects=True, vmem_limit_bytes=56 * 2**20
        ),
    )(hidden, out_embed, key_proj, targets, doc_ids, list_owner, list_block, list_count)
    return loss.reshape(768)


def solution(mesh):
    placed = (
        P("dp", None),
        P("dp", "vocab"),
        P(),
        P("dp"),
        P("dp"),
        P("dp", None),
        P("dp", None),
        P("dp"),
    )
    return jax.shard_map(per_device, mesh=mesh, in_specs=placed, out_specs=P("dp"), check_vma=False)
```

time: 89.3 us -> 86.4 us (0.968)
  Pallas kernels: 87.2 us -> 84.3 us
    pallas_call x1, Pallas kernels: 87.2 us -> 84.3 us  [per_device(): pl.pallas_call(kernel, out_shape=jax.ShapeDtypeStruct((6, 128), F32), in_...]
where the time goes in v2:
time: 86.4 us; the launch traced here: 86.3 us
  Pallas kernels  84.3 us (98%)
  local copies, waits for them, and re-layouts  1.28 us (1%)
    pallas_call x1, Pallas kernels, per_device(): pl.pallas_call(kernel, out_shape=jax.ShapeDtypeStruct((6, 128), F32), in_...  84.3 us

profile of v2, /device:TPU:1, one launch (start us, length us, event | category | flops | bytes accessed | tf_op | source)
XLA Modules:
  0.0 86.3 jit_solution(546389805794673268)
XLA Ops:
  0.7 84.3 %shard_map.82 = f32[6,128]{1,0:T(8,128)} custom-call(bf16[768,4096]{1,0:T(8,128)(2,1)} %hid.1, bf16[128,2048]{1,0:T(8,128)(2,1)} %emb.1, bf16[4096,128]{1,0:T(8,128)(2,1)} %kproj.1, s32[768]{0:T(1024)} %tgt.1, s32[768]{0:T(1024)} %doc.1, s32[1,64]{1,0:T(1,128)} %lown.1, s32[1,64]{1,0:T(1,128)} %lblk.1, s32[1]{0:T(128)S(6)} %copy.10.lcnt), custom_call_target="tpu_custom_call" | custom-call | tf_op jit(solution)/shard_map/pallas_call | solution.py:630
  85.0 1.3 %copy.11 = f32[768]{0:T(1024)} copy(f32[768]{0:T(1024)} %bitcast.1) | data formatting | bytes 6144

commit v3 on v2

--- a/solution.py
+++ b/solution.py
@@ -496,16 +496,18 @@
         def _():
             rr[y] = st[0]
 
-    for e in range(1, 4):
+    for e in (3, 2, 1):
         xe(0, e).start()
     z_first(0, 0)
     z_first(1, 0)
     x_send(0)
     x_send(1)
-    for e in range(1, 4):
+    small_sends()
+    x_send(2)
+    x_send(3)
+    for e in (3, 2, 1):
         xe(1, e).start()
-    small_sends()
-    for j in range(2, 12):
+    for j in range(4, 12):
         x_send(j)
     key_sends()
     z_first(0, 1)
@@ -522,17 +524,17 @@
         at(n, z_event, *ev)
     for hop, u in ((1, 0), (2, 2), (3, 4), (4, 5)):
         at(u, key_relay, hop)
-    at(3, z_first, 1, 1)
-    at(4, z_first, 1, 2)
-    for j, u in enumerate((-1, 1, 4, 5, 7, 8, 9, 10, 11, 12, 14, 14)):
+    at(4.6, z_first, 1, 1)
+    at(5.5, z_first, 1, 2)
+    for j, u in enumerate((-1, 1, 3, 4, 7, 8, 9, 9.4, 11, 12, 13.2, 13.2)):
         at(u, x_near, j)
-    for u, js in ((11, (4, 6)), (12, (5, 7)), (14, (8, 10)), (14, (9, 11))):
+    for u, js in ((9.45, (4, 6)), (10.5, (5, 7)), (13.3, (8, 10)), (13.3, (9, 11))):
         at(u, x_forward, *js)
-    for u, js in ((4, (0,)), (5, (1,)), (7, (2,)), (8, (3,)), (15, (4, 6)), (16, (5, 7)), (17, (8, 10)), (18, (9, 11))):
+    for u, js in ((4, (0,)), (5, (1,)), (6, (2,)), (8, (3,)), (13.3, (4, 6)), (13.3, (5, 7)), (17, (8, 10)), (18, (9, 11))):
         at(u, x_far, *js)
     for k in range(4):
-        at((6, 8, 10, 12)[k], y_near, k)
-        at((10, 11, 13, 14)[k], y_far, k)
+        at((6, 8, 9, 11.4)[k], y_near, k)
+        at((9, 10, 11.4, 12.4)[k], y_far, k)
         at((15, 17, 16, 18)[k], y_last, k)
     groups = [
         [jnp.where(first, a, b) for a, b in zip(on_first, on_second)]
@@ -547,19 +549,20 @@
     ]
     at(4, tokens_ready)
     at(7, memory_ready)
-    at(8, embed_ready, 0)
-    at(8, early, 0)
-    at(10, early, 1)
-    at(12, early, 2)
-    at(14, early, 3)
+    at(7.5, embed_ready, 0)
+    at(7.5, early, 0)
+    at(9.5, early, 1)
+    at(11.5, early, 2)
+    at(12.5, early, 3)
+    at(13.4, early, 4)
     at(14, embed_ready, 1)
     at(14, late, True, 0, 1)
     at(14, late, True, 2, 3)
-    at(16, late, False, 4)
+    at(15, late, True, 4)
     at(18, late, False, 5)
     at(17, most_results)
-    for u in range(-1, 22):
-        for fn, args in plan.get(u, []):
+    for u in sorted(plan):
+        for fn, args in plan[u]:
             fn(*args)
 
     for n in range(8):
@@ -646,8 +649,8 @@
             pltpu.VMEM((2, 8, 128), F32),
             pltpu.VMEM((2, 6, 128, 128), F32),
             pltpu.VMEM((2, 6, 128, 128), F32),
-            pltpu.VMEM((4, 2, 128, 128), F32),
-            pltpu.VMEM((4, 2, 128, 128), F32),
+            pltpu.VMEM((5, 2, 128, 128), F32),
+            pltpu.VMEM((5, 2, 128, 128), F32),
             pltpu.VMEM((2, 4, 8, 128), F32),
             pltpu.VMEM((2, 8, 128), F32),
             pltpu.VMEM((16, 4, 8, 128), F32),

time: 86.4 us -> 82.6 us (0.956)
  Pallas kernels: 84.3 us -> 80.5 us
    pallas_call x1, Pallas kernels: 84.3 us -> 80.5 us  [per_device(): pl.pallas_call(kernel, out_shape=jax.ShapeDtypeStruct((6, 128), F32), in_...]
where the time goes in v3:
time: 82.6 us; the launch traced here: 82.4 us
  Pallas kernels  80.5 us (97%)
  local copies, waits for them, and re-layouts  1.28 us (2%)
    pallas_call x1, Pallas kernels, per_device(): pl.pallas_call(kernel, out_shape=jax.ShapeDtypeStruct((6, 128), F32), in_...  80.5 us

profile of v3, /device:TPU:1, one launch (start us, length us, event | category | flops | bytes accessed | tf_op | source)
XLA Modules:
  0.0 82.4 jit_solution(7812399949740354528)
XLA Ops:
  0.7 80.5 %shard_map.82 = f32[6,128]{1,0:T(8,128)} custom-call(bf16[768,4096]{1,0:T(8,128)(2,1)} %hid.1, bf16[128,2048]{1,0:T(8,128)(2,1)} %emb.1, bf16[4096,128]{1,0:T(8,128)(2,1)} %kproj.1, s32[768]{0:T(1024)} %tgt.1, s32[768]{0:T(1024)} %doc.1, s32[1,64]{1,0:T(1,128)} %lown.1, s32[1,64]{1,0:T(1,128)} %lblk.1, s32[1]{0:T(128)S(6)} %copy.10.lcnt), custom_call_target="tpu_custom_call" | custom-call | tf_op jit(solution)/shard_map/pallas_call | solution.py:633
  81.2 1.3 %copy.11 = f32[768]{0:T(1024)} copy(f32[768]{0:T(1024)} %bitcast.1) | data formatting | bytes 6144

commit v4 on v3

--- a/solution.py
+++ b/solution.py
@@ -435,8 +435,8 @@
         return out_columns
 
     def early(n):
+        memory = score_tiles(n)
         columns = logit_columns(n, (0,))
-        memory = score_tiles(n)
         for h in range(2):
             sp[n, h] = lane_tile(8, columns[h])
             sm[n, h] = memory[h]
@@ -452,8 +452,8 @@
 
     def late_rows(n, was_early):
         i1 = lax.broadcasted_iota(jnp.int32, (128, 128), 1)
+        memory = [sm[n, 0], sm[n, 1]] if was_early else score_tiles(n)
         columns = logit_columns(n, (1,) if was_early else (0, 1))
-        memory = [sm[n, 0], sm[n, 1]] if was_early else score_tiles(n)
         rows = []
         for h, s, blk in halves(n):
             t = jnp.where(i1 < 4, lane_tile(0, columns[h]), memory[h])

time: 82.6 us -> 82.6 us (level)
  no operation moved by 1% of the time
where the time goes in v4:
time: 82.6 us; the launch traced here: 82.4 us
  Pallas kernels  80.5 us (97%)
  local copies, waits for them, and re-layouts  1.28 us (2%)
    pallas_call x1, Pallas kernels, per_device(): pl.pallas_call(kernel, out_shape=jax.ShapeDtypeStruct((6, 128), F32), in_...  80.5 us

profile of v4, /device:TPU:1, one launch (start us, length us, event | category | flops | bytes accessed | tf_op | source)
XLA Modules:
  0.0 82.4 jit_solution(5177620677538233838)
XLA Ops:
  0.7 80.5 %shard_map.82 = f32[6,128]{1,0:T(8,128)} custom-call(bf16[768,4096]{1,0:T(8,128)(2,1)} %hid.1, bf16[128,2048]{1,0:T(8,128)(2,1)} %emb.1, bf16[4096,128]{1,0:T(8,128)(2,1)} %kproj.1, s32[768]{0:T(1024)} %tgt.1, s32[768]{0:T(1024)} %doc.1, s32[1,64]{1,0:T(1,128)} %lown.1, s32[1,64]{1,0:T(1,128)} %lblk.1, s32[1]{0:T(128)S(6)} %copy.10.lcnt), custom_call_target="tpu_custom_call" | custom-call | tf_op jit(solution)/shard_map/pallas_call | solution.py:633
  81.1 1.3 %copy.11 = f32[768]{0:T(1024)} copy(f32[768]{0:T(1024)} %bitcast.1) | data formatting | bytes 6144
